TPU v7x, 32 devices: a whole 2x2x4 slice. The times are simulated.
32 devices in a mesh: seq: 4 (over y, x), head: 8 (over z, core).
Axes of the slice: x: 2, y: 2, z: 4, core: 2. Of those that a mesh axis runs over, the one named last changes fastest.
Arguments:
- tokens: bfloat16 [2048, 2048], P('seq'), may hold values from -40 to 40
- attention_gain: float32 [2048], replicated, may hold values from 0.1 to 1.9
- head_weights: bfloat16 [3, 2048, 2048], P(None, None, 'head'), may hold values from -1 to 1
- carried_state: float32 [8256, 2048], P(None, 'head'), may hold values from -384 to 384
- output_weight: bfloat16 [2048, 2048], P('head'), may hold values from -0.125 to 0.125
- expert_gain: float32 [2048], replicated, may hold values from 0.1 to 1.9
- router_weight: bfloat16 [2048, 64], replicated, may hold values from -0.125 to 0.125
- expert_index: int32 [2048, 8], P(('seq', 'head')), may hold values from 0 to 63, all different within a row; in each aligned block of 64 rows (0 to 63, 64 to 127, ...) at most 12 rows name the same one
- expert_first: bfloat16 [2, 2048, 65536], P(None, None, ('seq', 'head')), may hold values from -0.125 to 0.125
- expert_second: bfloat16 [65536, 2048], P(('seq', 'head')), may hold values from -0.1875 to 0.1875
Outputs:
- layer_out: bfloat16 [2048, 2048], P(('seq', 'head'))
Inputs may be any that keep to these rules, and one draw needn't show every extreme that they name: `expert_index`: each row names 8 different experts; within each aligned block of 64 rows (the rows of one device) no expert is named by more than 12 rows.
All inputs are finite; a program needn't handle non-finite values.
Results may differ from a plain program's by a relative error of at most 0.019.
Values may be sent and summed in bfloat16 or wider, within the bound.
A program may use at most 192 MiB of HBM per device.

v0:
```python
import math

import jax
import jax.numpy as jnp
import numpy as np
from jax import lax
from jax.sharding import PartitionSpec as P

HD = 128
EXPERTS = 64
TOP = 8


def partner_2(array, axis, apart):
    return lax.ppermute(array, axis, [(i, i ^ 1 << apart) for i in range(lax.axis_size(axis))])


def entering(array, axis, combine, identity):
    count, position = (lax.axis_size(axis), lax.axis_index(axis))
    everything = lax.all_gather(
        array.astype(jnp.bfloat16 if array.dtype == jnp.float32 else array.dtype), axis
    )
    start = jnp.broadcast_to(jnp.asarray(identity, array.dtype), array.shape)

    def hop(k, before):
        reached = k < position
        new = combine(before, everything[k].astype(array.dtype))
        return jnp.where(reached, new, before)

    return lax.fori_loop(0, count, hop, start)


def pair_tables(breadth):
    pair_rows = []
    pair_factor = []
    for first in range(breadth):
        for second in range(first, breadth):
            pair_rows.append(first * breadth + second)
            pair_factor.append(1.0 if first == second else math.sqrt(2.0))
    lookup = np.zeros((breadth, breadth), np.int32)
    spread = np.zeros((breadth, breadth), np.float32)
    place = 0
    for first in range(breadth):
        for second in range(first, breadth):
            lookup[first, second] = place
            lookup[second, first] = place
            spread[first, second] = 1.0 if first == second else math.sqrt(2.0) / 2.0
            spread[second, first] = spread[first, second]
            place += 1
    return (
        np.array(pair_rows, np.int32),
        np.array(pair_factor, np.float32),
        lookup.reshape(-1),
        spread.reshape(-1),
    )


def norm_scaled(values, gain):
    return values * lax.rsqrt(jnp.mean(values * values, axis=-1, keepdims=True) + 1e-06) * gain


def within_shard(query_rows, key_rows, value_rows):
    scores = lax.dot_general(
        query_rows, key_rows, (((1,), (1,)), ((), ())), preferred_element_type=jnp.float32
    )
    places = jnp.arange(query_rows.shape[0], dtype=jnp.int32)
    weights = jnp.where(places[None, :] <= places[:, None], scores * scores, 0.0)
    return jnp.dot(weights, value_rows.astype(jnp.float32), precision=lax.Precision.HIGHEST)


def build_state(key_rows, value_rows, block_rows):
    breadth = key_rows.shape[1]
    columns = value_rows.shape[1]

    def add_block(block_num, running):
        key_block = key_rows.astype(jnp.float32)
        value_block = value_rows.astype(jnp.float32)
        products = (key_block[:, :, None] * value_block[:, None, :]).reshape(
            block_rows, breadth * columns
        )
        return running + lax.dot_general(
            key_block, products, (((0,), (0,)), ((), ())), precision=lax.Precision.HIGHEST
        )

    initial = jnp.zeros((breadth, breadth * columns), jnp.float32)
    full_state = lax.fori_loop(0, key_rows.shape[0] // block_rows, add_block, initial).reshape(
        breadth * breadth, columns
    )
    pair_rows, pair_factor, lookup, spread = pair_tables(breadth)
    return jnp.take(full_state, jnp.asarray(pair_rows), axis=0) * jnp.asarray(pair_factor)[:, None]


def apply_state(query_rows, memory, block_rows):
    breadth = query_rows.shape[1]
    columns = memory.shape[1]
    pair_rows, pair_factor, lookup, spread = pair_tables(breadth)
    symmetric = (
        jnp.take(memory, jnp.asarray(lookup), axis=0) * jnp.asarray(spread)[:, None]
    ).reshape(breadth, breadth * columns)

    def one_block(block_num):
        query_block = query_rows.astype(jnp.float32)
        inner = jnp.dot(query_block, symmetric, precision=lax.Precision.HIGHEST).reshape(
            block_rows, breadth, columns
        )
        return jnp.sum(inner * query_block[:, :, None], axis=1)

    blocks = lax.map(one_block, jnp.arange(query_rows.shape[0] // block_rows, dtype=jnp.int32))
    return blocks.reshape(query_rows.shape[0], columns)


def add_pair(earlier, later):
    return earlier + later


def body(
    tokens,
    attention_gain,
    head_weights,
    carried_state,
    output_weight,
    expert_gain,
    router_weight,
    expert_index,
    expert_first,
    expert_second,
):
    shard_rows = tokens.shape[0]
    model_width = tokens.shape[1]
    block_rows = min(shard_rows, 512)
    floats = tokens.astype(jnp.float32)
    normed = norm_scaled(floats, attention_gain).astype(jnp.bfloat16)
    projected = jnp.einsum(
        "td,adc->atc", normed, head_weights, preferred_element_type=jnp.float32
    ).astype(jnp.bfloat16)
    query_rows, key_rows, value_rows = (projected[0], projected[1], projected[2])
    share = value_rows.shape[1]
    local_heads = max(1, share // HD)
    value_width = share // local_heads
    if value_width < HD:
        mine = jnp.stack([query_rows, key_rows])
        partner = partner_2(mine, "head", 0)
        lower = lax.axis_index("head") % 2 == 0
        joined = jnp.where(
            lower,
            jnp.concatenate([mine, partner], axis=2),
            jnp.concatenate([partner, mine], axis=2),
        )
        query_rows, key_rows = (joined[0], joined[1])

    def head_columns(head_num):
        return slice(head_num * HD, (head_num + 1) * HD)

    def value_columns(head_num):
        return slice(head_num * value_width, (head_num + 1) * value_width)

    raw_heads = []
    memories = jnp.stack(
        [
            build_state(
                key_rows[:, head_columns(head_num)],
                value_rows[:, value_columns(head_num)],
                block_rows,
            )
            for head_num in range(local_heads)
        ]
    )
    prefix = entering(memories, "seq", add_pair, jnp.zeros_like(memories))
    for head_num in range(local_heads):
        nearby = within_shard(
            query_rows[:, head_columns(head_num)],
            key_rows[:, head_columns(head_num)],
            value_rows[:, value_columns(head_num)],
        )
        carried = apply_state(
            query_rows[:, head_columns(head_num)],
            carried_state[:, value_columns(head_num)] + prefix[head_num],
            block_rows,
        )
        raw_heads.append((nearby + carried) / HD)
    raw_stack = jnp.stack(raw_heads)
    squares = jnp.sum(raw_stack * raw_stack, axis=2, keepdims=True)
    if value_width < HD:
        squares = squares + partner_2(squares, "head", 0)
    scaled_heads = (raw_stack * lax.rsqrt(squares / HD + 1e-06)).astype(jnp.bfloat16)
    attended = scaled_heads.transpose(1, 0, 2).reshape(shard_rows, share)
    slab_rows = expert_index.shape[0]
    attention_sum = lax.psum_scatter(
        jnp.dot(attended, output_weight, preferred_element_type=jnp.float32).astype(jnp.bfloat16),
        "head",
        scatter_dimension=0,
        tiled=True,
    ).astype(jnp.float32)
    token_slab = lax.dynamic_slice_in_dim(floats, lax.axis_index("head") * slab_rows, slab_rows, 0)
    residual = token_slab + attention_sum
    expert_input = norm_scaled(residual, expert_gain).astype(jnp.bfloat16)
    logits = jnp.dot(expert_input, router_weight, preferred_element_type=jnp.float32)
    matches = expert_index[:, :, None] == jnp.arange(EXPERTS, dtype=jnp.int32)
    gate_values = jax.nn.sigmoid(jnp.sum(jnp.where(matches, logits[:, None, :], 0.0), axis=2))
    flat_matches = matches.reshape(slab_rows * TOP, EXPERTS).astype(jnp.int32)
    earlier = jnp.cumsum(flat_matches, axis=0) - flat_matches
    slots = jnp.sum(earlier * flat_matches, axis=1).reshape(slab_rows, TOP)
    devices = lax.axis_size("seq") * lax.axis_size("head")
    piece_count = max(1, devices // EXPERTS)
    local_experts = max(1, EXPERTS // devices)
    capacity = max(2, 3 * slab_rows * TOP // (2 * EXPERTS))
    groups = EXPERTS * piece_count
    targets = (slots * groups + expert_index * piece_count)[:, :, None] + jnp.arange(
        piece_count, dtype=jnp.int32
    )
    send_map = jnp.sum(
        (
            targets.reshape(slab_rows, TOP * piece_count, 1)
            == jnp.arange(capacity * groups, dtype=jnp.int32)
        ).astype(jnp.bfloat16),
        axis=1,
    )
    outgoing = (
        lax.dot_general(
            send_map, expert_input, (((0,), (0,)), ((), ())), preferred_element_type=jnp.float32
        )
        .astype(jnp.bfloat16)
        .reshape(capacity, groups, model_width)
    )
    cells = capacity * EXPERTS
    combine_map = jnp.sum(
        jnp.where(
            (slots * EXPERTS + expert_index)[:, :, None] == jnp.arange(cells, dtype=jnp.int32),
            gate_values[:, :, None],
            0.0,
        ),
        axis=1,
    )
    piece_width = expert_first.shape[2] // local_experts
    first_local = expert_first.reshape(2, model_width, local_experts, piece_width)
    second_local = expert_second.reshape(local_experts, piece_width, model_width)
    arrived = lax.all_to_all(outgoing, ("seq", "head"), split_axis=1, concat_axis=1, tiled=True)
    slot_count = arrived.shape[0]
    grouped = arrived.reshape(slot_count, devices, local_experts, model_width)
    paired = jnp.einsum(
        "ksed,gdef->gksef", grouped, first_local, preferred_element_type=jnp.float32
    )
    hidden = (jax.nn.silu(paired[0]) * paired[1]).astype(jnp.bfloat16)
    produced = jnp.einsum(
        "ksef,efd->ksed", hidden, second_local, preferred_element_type=jnp.float32
    ).astype(jnp.bfloat16)
    returned = lax.all_to_all(
        produced.reshape(slot_count, devices * local_experts, model_width),
        ("seq", "head"),
        split_axis=1,
        concat_axis=1,
        tiled=True,
    )
    summed = jnp.sum(
        returned.reshape(capacity, EXPERTS, piece_count, model_width).astype(jnp.float32), axis=2
    )
    expert_sum = jnp.dot(
        combine_map, summed.reshape(cells, model_width), precision=lax.Precision.HIGHEST
    )
    return (residual + expert_sum).astype(jnp.bfloat16)


def solution(mesh):
    in_specs = (
        P("seq", None),
        P(),
        P(None, None, "head"),
        P(None, "head"),
        P("head", None),
        P(),
        P(),
        P(("seq", "head"), None),
        P(None, None, ("seq", "head")),
        P(("seq", "head"), None),
    )
    out_specs = P(("seq", "head"), None)
    return jax.shard_map(body, mesh=mesh, in_specs=in_specs, out_specs=out_specs, check_vma=False)
```

profile of v0, /device:TPU:0, one launch (start us, length us, event | category | flops | bytes accessed | tf_op | source)
XLA Modules:
  0.0 887.9 jit_solution(9013946222821150400)
XLA Ops:
  12.7 11.4 %broadcast_multiply_fusion.1 = f32[512,128,128]{2,1,0:T(8,128)} fusion(f32[512,128]{1,0:T(8,128)S(1)} %get-tuple-element.167, f32[512,128]{1,0:T(8,128)S(1)} %get-tuple-element.174), kind=kLoop, calls=%fused_computation.16 | loop fusion | flops 8388608 | bytes 34078720 | tf_op jit(solution)/shard_map/while/body/eval_jaxpr/mul | solution.py:78
  24.1 45.0 %fusion.3 = f32[128,16384]{1,0:T(8,128)} fusion(f32[64,8,128,128]{3,2,1,0:T(8,128)} %bitcast.116, bf16[512,256]{1,0:T(8,128)(2,1)S(1)} %get-tuple-element.160), kind=kOutput, calls=%fused_computation.8 | convolution fusion | flops 12884901888 | bytes 42074112 | tf_op jit(solution)/shard_map/while/body/eval_jaxpr/dot_general | solution.py:81
  69.1 9.2 %reshape.167 = f32[16384,128]{1,0:T(8,128)} reshape(f32[128,16384]{1,0:T(8,128)} %fusion.3) | data formatting | bytes 16777216 | tf_op jit(solution)/shard_map/reshape | solution.py:86
  78.4 11.4 %broadcast_multiply_fusion = f32[512,128,128]{2,1,0:T(8,128)} fusion(f32[512,128]{1,0:T(8,128)S(1)} %get-tuple-element.168, f32[512,128]{1,0:T(8,128)S(1)} %get-tuple-element.173), kind=kLoop, calls=%fused_computation.15 | loop fusion | flops 8388608 | bytes 34078720 | tf_op jit(solution)/shard_map/while/body/eval_jaxpr/mul | solution.py:78
  89.8 45.2 %fusion = f32[128,16384]{1,0:T(8,128)} fusion(f32[64,8,128,128]{3,2,1,0:T(8,128)} %bitcast.117, bf16[512,256]{1,0:T(8,128)(2,1)S(1)} %get-tuple-element.160), kind=kOutput, calls=%fused_computation.5 | convolution fusion | flops 12884901888 | bytes 42074112 | tf_op jit(solution)/shard_map/while/body/eval_jaxpr/dot_general | solution.py:81
  135.0 9.3 %reshape.168 = f32[16384,128]{1,0:T(8,128)} reshape(f32[128,16384]{1,0:T(8,128)} %fusion) | data formatting | bytes 16777216 | tf_op jit(solution)/shard_map/reshape | solution.py:86
  144.2 19.6 %gather_fusion = f32[8256,128]{1,0:T(8,128)} fusion(f32[16384,128]{1,0:T(8,128)} %reshape.167, s32[9216]{0:T(1024)S(1)} %pad_clamp_fusion), kind=kCustom, calls=%fused_computation.clone | custom fusion | bytes 8487168 | tf_op jit(solution)/shard_map/jit(_take)/gather | solution.py:90
  163.8 19.7 %gather_fusion.1 = f32[8256,128]{1,0:T(8,128)} fusion(f32[16384,128]{1,0:T(8,128)} %reshape.168, s32[9216]{0:T(1024)S(1)} %pad_clamp_fusion), kind=kCustom, calls=%fused_computation.2.clone | custom fusion | bytes 8487168 | tf_op jit(solution)/shard_map/jit(_take)/gather | solution.py:90
  193.1 160.9 %all-gather.2.cloned.1.call-done = bf16[4,2,8256,128]{3,2,1,0:T(8,128)(2,1)} async-done(((bf16[1,2,8256,128]{3,2,1,0:T(8,128)(2,1)}), bf16[4,2,8256,128]{3,2,1,0:T(8,128)(2,1)}) %all-gather.2.cloned.1.call-update) | async-done | bytes 16908304 | tf_op jit(solution)/shard_map/all_gather | solution.py:20
  354.0 29.3 %while.9 = (s32[]{:T(128)}, f32[2,8256,128]{2,1,0:T(8,128)}, s32[]{:T(128)}, bf16[4,2,8256,128]{3,2,1,0:T(8,128)(2,1)}, s32[]{:T(128)}, /*index=5*/s32[]{:T(128)}) while((s32[]{:T(128)}, f32[2,8256,128]{2,1,0:T(8,128)}, s32[]{:T(128)}, bf16[4,2,8256,128]{3,2,1,0:T(8,128)(2,1)}, s32[]{:T(128)}, /*index=5*/s32[]{:T(128)}) %tuple.52), condition=%wide.region_2.4_spmd.clone, body=%wide.region_1.3_spmd.clone.sunk | while | flops 8454148 | bytes 21135452 | solution.py:30
  383.3 9.9 %bitcast_add_fusion.1 = (f32[8256,128]{1,0:T(8,128)}, f32[8256,128]{1,0:T(8,128)}) fusion(f32[2,8256,128]{2,1,0:T(8,128)} %get-tuple-element.134, f32[8256,256]{1,0:T(8,128)} %param.27), kind=kLoop, calls=%fused_computation.19 | loop fusion | flops 2113536 | bytes 25362432 | tf_op jit(solution)/shard_map/add | solution.py:177
  393.2 56.6 %gather_fusion.2 = f32[16384,128]{1,0:T(8,128)} fusion(f32[8256,128]{1,0:T(8,128)} %get-tuple-element.158, s32[16384]{0:T(1024)S(1)} %broadcast_clamp_fusion), kind=kCustom, calls=%fused_computation.1.clone | custom fusion | bytes 16842752 | tf_op jit(solution)/shard_map/jit(_take)/gather | solution.py:98
  449.8 56.6 %gather_fusion.3 = f32[16384,128]{1,0:T(8,128)} fusion(f32[8256,128]{1,0:T(8,128)} %get-tuple-element.159, s32[16384]{0:T(1024)S(1)} %broadcast_clamp_fusion), kind=kCustom, calls=%fused_computation.3.clone | custom fusion | bytes 16842752 | tf_op jit(solution)/shard_map/jit(_take)/gather | solution.py:98
  506.4 15.9 %broadcast_multiply_fusion.3 = (f32[16384,128]{1,0:T(8,128)}, f32[16384,128]{1,0:T(8,128)}) fusion(f32[16384,128]{1,0:T(8,128)} %gather_fusion.2, f32[16384]{0:T(1024)S(1)} %copy-done.12, f32[16384,128]{1,0:T(8,128)} %gather_fusion.3), kind=kLoop, calls=%fused_computation.23 | loop fusion | flops 4194304 | bytes 33619968 | tf_op jit(solution)/shard_map/mul | solution.py:98
  522.3 9.4 %reshape.169 = f32[128,16384]{1,0:T(8,128)} reshape(f32[16384,128]{1,0:T(8,128)} %get-tuple-element.169) | data formatting | bytes 16777216 | tf_op jit(solution)/shard_map/reshape | solution.py:99
  540.7 17.4 %multiply_reduce_fusion.1 = f32[512,128]{1,0:T(8,128)S(1)} fusion(f32[512,128]{0,1:T(8,128)S(1)} %copy.97, f32[128,128,128]{2,1,0:T(8,128)} %bitcast.125, bf16[512,256]{1,0:T(8,128)(2,1)S(1)} %get-tuple-element.162), kind=kOutput, calls=%fused_computation.12 | convolution fusion | flops 12901613568 | bytes 9043968 | tf_op jit(solution)/shard_map/while/body/eval_jaxpr/dot_general | solution.py:103
  558.3 9.4 %reshape.170 = f32[128,16384]{1,0:T(8,128)} reshape(f32[16384,128]{1,0:T(8,128)} %get-tuple-element.170) | data formatting | bytes 16777216 | tf_op jit(solution)/shard_map/reshape | solution.py:99
  567.7 9.0 %copy.99 = f32[16384,128]{1,0:T(8,128)} copy(f32[16384,128]{0,1:T(8,128)} %bitcast.119) | data formatting | bytes 16777216 | tf_op jit(solution)/shard_map/while/body/eval_jaxpr/dot_general | solution.py:103
  576.7 18.2 %multiply_reduce_fusion = f32[512,128]{1,0:T(8,128)} fusion(f32[512,128]{0,1:T(8,128)S(1)} %copy-done.11, f32[128,128,128]{2,1,0:T(8,128)} %bitcast.124, bf16[512,256]{1,0:T(8,128)(2,1)S(1)} %get-tuple-element.162), kind=kOutput, calls=%fused_computation.11 | convolution fusion | flops 12901613568 | bytes 9043968 | tf_op jit(solution)/shard_map/while/body/eval_jaxpr/dot_general | solution.py:103
  606.5 30.8 %reduce-scatter.2.cloned.1.call-done = bf16[64,2048]{1,0:T(8,128)(2,1)} async-done(((bf16[512,2048]{1,0:T(8,128)(2,1)}), bf16[64,2048]{1,0:T(8,128)(2,1)}) %reduce-scatter.2.cloned.1.call-update) | async-done | bytes 262160 | tf_op jit(solution)/shard_map/reduce_scatter | solution.py:188
  648.9 27.7 %reshape.175 = bf16[2,2048,2,1024]{3,2,1,0:T(2,128)(2,1)} reshape(bf16[2,2048,2048]{2,1,0:T(8,128)(2,1)} %param.32) | data formatting | bytes 33554432 | tf_op jit(solution)/shard_map/reshape | solution.py:235
  676.6 67.4 %all-to-all-done = bf16[12,64,2048]{2,0,1:T(8,128)(2,1)} async-done(((bf16[12,64,2048]{2,0,1:T(8,128)(2,1)}), bf16[12,64,2048]{2,0,1:T(8,128)(2,1)}, u32[]{:S(2)}, u32[]{:S(2)}) %all-to-all-start) | async-done | bytes 3145760 | tf_op jit(solution)/shard_map/all_to_all | solution.py:237
  744.0 19.5 %fusion.12 = f32[2,12,32,2,1024]{4,2,0,1,3:T(8,128)S(1)} fusion(bf16[2,2048,2,1024,1]{3,2,1,0,4:T(2,128)(2,1)} %bitcast.121, bf16[12,32,2,2048,1]{3,0,2,1,4:T(8,128)(2,1)} %bitcast.22), kind=kOutput, calls=%fused_computation.35 | convolution fusion | flops 6442450944 | bytes 26214400 | tf_op jit(solution)/shard_map/ksed,gdef->gksef/dot_general | solution.py:240
  780.2 93.2 %all-to-all-done.1 = bf16[12,64,2048]{2,0,1:T(8,128)(2,1)} async-done(((bf16[12,64,2048]{2,0,1:T(8,128)(2,1)}), bf16[12,64,2048]{2,0,1:T(8,128)(2,1)}, u32[]{:S(2)}, u32[]{:S(2)}) %all-to-all-start.1) | async-done | bytes 3145760 | tf_op jit(solution)/shard_map/all_to_all | solution.py:247
  (99 shorter events, 100.8 us)
Async XLA Ops:
  6.5 2.5 copy-start
  6.5 347.5 %all-gather.2.cloned.1.call-start = ((), (), s32[]{:S(2)}) async-start(), calls=%async_computation.3 | async-start | bytes 21135360 | tf_op jit(solution)/shard_map/all_gather | solution.py:20
  12.6 11.5 %copy-start.6 = (bf16[512,256]{1,0:T(8,128)(2,1)}, bf16[512,256]{1,0:T(8,128)(2,1)S(1)}, u32[]{:S(2)}) copy-start(bf16[512,256]{1,0:T(8,128)(2,1)S(1)} %get-tuple-element.161) | copy-start | bytes 786436
  69.1 9.2 %copy-start.15 = (s32[8256]{0:T(1024)S(1)}, s32[8256]{0:T(1024)}, u32[]{:S(2)}) copy-start(s32[8256]{0:T(1024)} %constant.156) | copy-start | bytes 99076
  163.8 19.7 %copy-start.14 = (f32[8256]{0:T(1024)S(1)}, f32[8256]{0:T(1024)}, u32[]{:S(2)}) copy-start(f32[8256]{0:T(1024)} %constant.117.clone) | copy-start | bytes 99076
  191.4 1.7 copy-start.13
  191.4 445.9 %reduce-scatter.2.cloned.1.call-start = ((), (), s32[]{:S(2)}) async-start(), calls=%async_computation.4 | async-start | bytes 2359296 | tf_op jit(solution)/shard_map/reduce_scatter | solution.py:188
  449.8 56.6 %copy-start.12 = (f32[16384]{0:T(1024)S(1)}, f32[16384]{0:T(1024)}, u32[]{:S(2)}) copy-start(f32[16384]{0:T(1024)} %constant.119.clone) | copy-start | bytes 196612
  567.7 9.0 %copy-start.11 = (f32[512,128]{0,1:T(8,128)S(1)}, f32[512,128]{0,1:T(8,128)}, u32[]{:S(2)}) copy-start(f32[512,128]{0,1:T(8,128)} %copy.100) | copy-start | bytes 786436
  576.7 19.9 %copy-start.7 = (bf16[512,256]{1,0:T(8,128)(2,1)S(1)}, bf16[512,256]{1,0:T(8,128)(2,1)}, u32[]{:S(2)}) copy-start(bf16[512,256]{1,0:T(8,128)(2,1)} %copy-done.6) | copy-start | bytes 786436
  596.7 2.5 copy-start.8
  599.0 2.3 copy-start.2
  601.3 2.5 copy-start.17
  601.3 37.3 %copy-start.16 = (f32[2048]{0:T(1024)S(1)}, f32[2048]{0:T(1024)}, u32[]{:S(2)}) copy-start(f32[2048]{0:T(1024)} %param.29) | copy-start | bytes 24580
  639.9 0.7 copy-start.4
  645.3 98.6 %all-to-all-start = ((bf16[12,64,2048]{2,0,1:T(8,128)(2,1)}), bf16[12,64,2048]{2,0,1:T(8,128)(2,1)}, u32[]{:S(2)}, u32[]{:S(2)}) async-start(bf16[12,64,2048]{2,0,1:T(8,128)(2,1)} %copy.109), calls=%async_computation.1 | async-start | bytes 8388608 | tf_op jit(solution)/shard_map/all_to_all | solution.py:237
  774.4 3.9 copy-start.5
  774.4 3.9 copy-start.10
  774.4 99.0 %all-to-all-start.1 = ((bf16[12,64,2048]{2,0,1:T(8,128)(2,1)}), bf16[12,64,2048]{2,0,1:T(8,128)(2,1)}, u32[]{:S(2)}, u32[]{:S(2)}) async-start(bf16[12,64,2048]{2,0,1:T(8,128)(2,1)} %bitcast.120), calls=%async_computation.2 | async-start | bytes 8388608 | tf_op jit(solution)/shard_map/all_to_all | solution.py:247
  778.3 99.0 %copy-start.3 = (bf16[64,2048]{1,0:T(8,128)(2,1)S(1)}, bf16[64,2048]{1,0:T(8,128)(2,1)}, u32[]{:S(2)}) copy-start(bf16[64,2048]{1,0:T(8,128)(2,1)} %reduce-scatter.2.cloned.1.call-done) | copy-start | bytes 786436
  779.0 101.9 %copy-start.1 = (bf16[3,2048,256]{2,1,0:T(8,128)(2,1)S(1)}, bf16[3,2048,256]{2,1,0:T(8,128)(2,1)}, u32[]{:S(2)}) copy-start(bf16[3,2048,256]{2,1,0:T(8,128)(2,1)} %param.26) | copy-start | bytes 9437188
  873.4 4.0 copy-start.9
Sparse Core Ops, SparseCore 0:
  191.5 162.4 all-gather.1
  601.5 35.7 reduce-scatter.1
where the time goes:
time: 898 us; the launch traced here: 888 us
  waiting for transfers between devices  352 us (39%)
  local copies, waits for them, and re-layouts  252 us (28%)
  matrix products  166 us (18%)
  other arithmetic  96.4 us (11%)
  between operations  14 us (2%)
    all_gather x1, waiting for transfers between devices, entering(): lax.all_gather(array.astype(jnp.bfloat16 if array.dtype == jnp.float32 el...  161 us
    gather x2, local copies, waits for them, and re-layouts, apply_state(): jnp.take(memory, jnp.asarray(lookup), axis=0) * jnp.asarray(spread)[:, None]  113 us
    all_to_all x1, waiting for transfers between devices, body(): lax.all_to_all(produced.reshape(slot_count, devices * local_experts, mode...  93.2 us
    dot_general x2, matrix products, add_block(): lax.dot_general(key_block, products, (((0,), (0,)), ((), ())), precision=...  90.2 us
    all_to_all x1, waiting for transfers between devices, body(): lax.all_to_all(outgoing, ('seq', 'head'), split_axis=1, concat_axis=1, ti...  67.4 us
    gather x2, local copies, waits for them, and re-layouts, build_state(): jnp.take(full_state, jnp.asarray(pair_rows), axis=0)  39.3 us
    dot_general x2, matrix products, one_block(): jnp.dot(query_block, symmetric, precision=lax.Precision.HIGHEST)  35.6 us
    reduce_scatter x1, waiting for transfers between devices, body(): lax.psum_scatter(jnp.dot(attended, output_weight, preferred_element_type=...  30.8 us
  transfers between devices with their start and end apart: 4, of which 4 were waited for; matrix products, arithmetic and copies ran while one was open for 4% of the time, Pallas kernels for 0%

commit v1 on v0

v1 whole, which is shorter than its diff:
```python
import functools
import math

import jax
import jax.numpy as jnp
from jax import lax
from jax.experimental import pallas as pl
from jax.experimental.pallas import tpu as pltpu
from jax.sharding import PartitionSpec as P

HD = 128
EXPERTS = 64
TOP = 8


def partner_2(array, axis, apart):
    return lax.ppermute(array, axis, [(i, i ^ 1 << apart) for i in range(lax.axis_size(axis))])


def norm_scaled(values, gain):
    return values * lax.rsqrt(jnp.mean(values * values, axis=-1, keepdims=True) + 1e-06) * gain


def carried_kernel(breadth, heads, width, q_ref, memory_ref, out_ref, slab_ref):
    group = 16
    tokens = q_ref.shape[1]
    part = min(256, tokens)
    out_ref[...] = jnp.zeros_like(out_ref)
    place = lax.broadcasted_iota(jnp.int32, (breadth, heads * width), 0)

    def step(a, carry):
        for b in range(group):
            i = a * group + b
            fixed = (breadth - 1) * b - b * (b - 1) // 2
            shift = fixed % 8
            base = (
                a * (group * (breadth - 1) + group // 2)
                - a * a * (group * group // 2)
                - a * (group * b)
                + (fixed - shift)
            )
            rows = breadth + 8 if shift else breadth
            slab = memory_ref[pl.ds(pl.multiple_of(base, 8), rows), :]
            slab = slab[shift : shift + breadth]
            factor = jnp.where(place > i, math.sqrt(2.0), jnp.where(place == i, 1.0, 0.0))
            slab_ref[b] = (slab * factor).T.astype(jnp.bfloat16)
        for head in range(heads):
            q_rows = q_ref[pl.ds(pl.multiple_of(head * breadth + a * group, group), group), :]
            for first in range(0, tokens, part):
                columns = slice(first, first + part)
                weights = q_ref[head * breadth : (head + 1) * breadth, columns].astype(jnp.bfloat16)
                total = out_ref[head * width : (head + 1) * width, columns]
                for b in range(group):
                    inner = jnp.dot(
                        slab_ref[b, head * width : (head + 1) * width, :],
                        weights,
                        preferred_element_type=jnp.float32,
                    )
                    total = total + inner * q_rows[b : b + 1, columns]
                out_ref[head * width : (head + 1) * width, columns] = total
        return carry

    lax.fori_loop(0, breadth // group, step, 0)


def apply_carried(q_t, memory, heads, width):
    tokens = q_t.shape[1]
    return pl.pallas_call(
        functools.partial(carried_kernel, HD, heads, width),
        out_shape=jax.ShapeDtypeStruct((heads * width, tokens), jnp.float32),
        in_specs=[pl.BlockSpec(memory_space=pltpu.VMEM)] * 2,
        out_specs=pl.BlockSpec(memory_space=pltpu.VMEM),
        scratch_shapes=[pltpu.VMEM((16, heads * width, HD), jnp.bfloat16)],
        compiler_params=pltpu.CompilerParams(vmem_limit_bytes=40 * 2**20),
        cost_estimate=pl.CostEstimate(
            flops=4 * heads * width * HD * HD * tokens,
            bytes_accessed=memory.size * 4,
            transcendentals=0,
        ),
        name="carried_state",
    )(q_t, memory)


def causal_kernel(heads, width, me_ref, q_ref, keys_ref, values_ref, carried_ref, out_ref):
    shards, rows, _ = keys_ref.shape
    tokens = q_ref.shape[1]
    mine = me_ref[0]
    key_place = lax.broadcasted_iota(jnp.int32, (rows, tokens), 0)
    query_place = lax.broadcasted_iota(jnp.int32, (rows, tokens), 1) + mine * rows
    out_ref[...] = carried_ref[...]

    def shard_step(shard, carry):
        visible = key_place + shard * rows <= query_place
        for head in range(heads):
            scores = jnp.dot(
                keys_ref[shard, :, head * HD : (head + 1) * HD],
                q_ref[head * HD : (head + 1) * HD, :].astype(jnp.bfloat16),
                preferred_element_type=jnp.float32,
            )
            weights = jnp.where(visible, scores * scores, 0.0).astype(jnp.bfloat16)
            out_ref[head * width : (head + 1) * width, :] += lax.dot_general(
                values_ref[shard, :, head * width : (head + 1) * width],
                weights,
                (((0,), (0,)), ((), ())),
                preferred_element_type=jnp.float32,
            )
        return carry

    lax.fori_loop(0, mine + 1, shard_step, 0)


def causal_rows(q_t, keys, values, carried, heads, width):
    return pl.pallas_call(
        functools.partial(causal_kernel, heads, width),
        out_shape=jax.ShapeDtypeStruct(carried.shape, jnp.float32),
        in_specs=[pl.BlockSpec(memory_space=pltpu.SMEM)]
        + [pl.BlockSpec(memory_space=pltpu.VMEM)] * 4,
        out_specs=pl.BlockSpec(memory_space=pltpu.VMEM),
        compiler_params=pltpu.CompilerParams(vmem_limit_bytes=40 * 2**20),
        name="causal_scores",
    )(lax.axis_index("seq").astype(jnp.int32).reshape(1), q_t, keys, values, carried)


def body(
    tokens,
    attention_gain,
    head_weights,
    carried_state,
    output_weight,
    expert_gain,
    router_weight,
    expert_index,
    expert_first,
    expert_second,
):
    shard_rows = tokens.shape[0]
    model_width = tokens.shape[1]
    floats = tokens.astype(jnp.float32)
    normed = norm_scaled(floats, attention_gain).astype(jnp.bfloat16)
    projected = jnp.einsum(
        "td,adc->atc", normed, head_weights, preferred_element_type=jnp.float32
    ).astype(jnp.bfloat16)
    query_rows, key_rows, value_rows = (projected[0], projected[1], projected[2])
    share = value_rows.shape[1]
    local_heads = max(1, share // HD)
    value_width = share // local_heads
    if value_width < HD:
        mine = jnp.stack([query_rows, key_rows])
        partner = partner_2(mine, "head", 0)
        lower = lax.axis_index("head") % 2 == 0
        joined = jnp.where(
            lower,
            jnp.concatenate([mine, partner], axis=2),
            jnp.concatenate([partner, mine], axis=2),
        )
        query_rows, key_rows = (joined[0], joined[1])

    gathered = lax.all_gather(jnp.concatenate([key_rows, value_rows], axis=1), "seq")
    key_width = key_rows.shape[1]
    q_t = query_rows.T.astype(jnp.float32)
    carried = apply_carried(q_t, carried_state, local_heads, value_width)
    raw_t = causal_rows(
        q_t,
        gathered[:, :, :key_width],
        gathered[:, :, key_width:],
        carried,
        local_heads,
        value_width,
    ).reshape(local_heads, value_width, shard_rows) / HD
    squares = jnp.sum(raw_t * raw_t, axis=1, keepdims=True)
    if value_width < HD:
        squares = squares + partner_2(squares, "head", 0)
    scaled_heads = (raw_t * lax.rsqrt(squares / HD + 1e-06)).astype(jnp.bfloat16)
    attended = scaled_heads.reshape(share, shard_rows).T
    slab_rows = expert_index.shape[0]
    attention_sum = lax.psum_scatter(
        jnp.dot(attended, output_weight, preferred_element_type=jnp.float32).astype(jnp.bfloat16),
        "head",
        scatter_dimension=0,
        tiled=True,
    ).astype(jnp.float32)
    token_slab = lax.dynamic_slice_in_dim(floats, lax.axis_index("head") * slab_rows, slab_rows, 0)
    residual = token_slab + attention_sum
    expert_input = norm_scaled(residual, expert_gain).astype(jnp.bfloat16)
    logits = jnp.dot(expert_input, router_weight, preferred_element_type=jnp.float32)
    matches = expert_index[:, :, None] == jnp.arange(EXPERTS, dtype=jnp.int32)
    gate_values = jax.nn.sigmoid(jnp.sum(jnp.where(matches, logits[:, None, :], 0.0), axis=2))
    flat_matches = matches.reshape(slab_rows * TOP, EXPERTS).astype(jnp.int32)
    earlier = jnp.cumsum(flat_matches, axis=0) - flat_matches
    slots = jnp.sum(earlier * flat_matches, axis=1).reshape(slab_rows, TOP)
    devices = lax.axis_size("seq") * lax.axis_size("head")
    piece_count = max(1, devices // EXPERTS)
    local_experts = max(1, EXPERTS // devices)
    capacity = max(2, 3 * slab_rows * TOP // (2 * EXPERTS))
    groups = EXPERTS * piece_count
    targets = (slots * groups + expert_index * piece_count)[:, :, None] + jnp.arange(
        piece_count, dtype=jnp.int32
    )
    send_map = jnp.sum(
        (
            targets.reshape(slab_rows, TOP * piece_count, 1)
            == jnp.arange(capacity * groups, dtype=jnp.int32)
        ).astype(jnp.bfloat16),
        axis=1,
    )
    outgoing = (
        lax.dot_general(
            send_map, expert_input, (((0,), (0,)), ((), ())), preferred_element_type=jnp.float32
        )
        .astype(jnp.bfloat16)
        .reshape(capacity, groups, model_width)
    )
    cells = capacity * EXPERTS
    combine_map = jnp.sum(
        jnp.where(
            (slots * EXPERTS + expert_index)[:, :, None] == jnp.arange(cells, dtype=jnp.int32),
            gate_values[:, :, None],
            0.0,
        ),
        axis=1,
    )
    piece_width = expert_first.shape[2] // local_experts
    first_local = expert_first.reshape(2, model_width, local_experts, piece_width)
    second_local = expert_second.reshape(local_experts, piece_width, model_width)
    arrived = lax.all_to_all(outgoing, ("seq", "head"), split_axis=1, concat_axis=1, tiled=True)
    slot_count = arrived.shape[0]
    grouped = arrived.reshape(slot_count, devices, local_experts, model_width)
    paired = jnp.einsum(
        "ksed,gdef->gksef", grouped, first_local, preferred_element_type=jnp.float32
    )
    hidden = (jax.nn.silu(paired[0]) * paired[1]).astype(jnp.bfloat16)
    produced = jnp.einsum(
        "ksef,efd->ksed", hidden, second_local, preferred_element_type=jnp.float32
    ).astype(jnp.bfloat16)
    returned = lax.all_to_all(
        produced.reshape(slot_count, devices * local_experts, model_width),
        ("seq", "head"),
        split_axis=1,
        concat_axis=1,
        tiled=True,
    )
    summed = jnp.sum(
        returned.reshape(capacity, EXPERTS, piece_count, model_width).astype(jnp.float32), axis=2
    )
    expert_sum = jnp.dot(
        combine_map, summed.reshape(cells, model_width), precision=lax.Precision.HIGHEST
    )
    return (residual + expert_sum).astype(jnp.bfloat16)


def solution(mesh):
    in_specs = (
        P("seq", None),
        P(),
        P(None, None, "head"),
        P(None, "head"),
        P("head", None),
        P(),
        P(),
        P(("seq", "head"), None),
        P(None, None, ("seq", "head")),
        P(("seq", "head"), None),
    )
    out_specs = P(("seq", "head"), None)
    return jax.shard_map(body, mesh=mesh, in_specs=in_specs, out_specs=out_specs, check_vma=False)
```

time: 898 us -> 349 us (0.39); the launches traced: 888 us -> 348 us
  local copies, waits for them, and re-layouts: 252 us -> 49.6 us
  waiting for transfers between devices: 352 us -> 214 us
  matrix products: 166 us -> 37 us
  other arithmetic: 96.4 us -> 11.7 us
  Pallas kernels: 0 us -> 14.4 us
    gather x4 -> x0, local copies, waits for them, and re-layouts: 153 us -> none  [the longest x2 113 us: apply_state(): jnp.take(memory, jnp.asarray(lookup), axis=0) * jnp.asarray(spread)[:, None]]
    all_gather x1, waiting for transfers between devices: 161 us -> 21 us  [body(): lax.all_gather(jnp.concatenate([key_rows, value_rows], axis=1), 'seq')]
    dot_general x8 -> x0, matrix products: 129 us -> none  [the longest x2 90.2 us: add_block(): lax.dot_general(key_block, products, (((0,), (0,)), ((), ())), precision=...]
    mul x3 -> x1, other arithmetic: 38.8 us -> 0.01 us  [body(): raw_t * lax.rsqrt(squares / HD + 1e-06)]
    reshape x4 -> x0, local copies, waits for them, and re-layouts: 37.3 us -> none  [the longest x2 18.8 us: apply_state(): symmetric = (jnp.take(memory, jnp.asarray(lookup), axis=0) * jnp.asarray(...]
    select_n x4 -> x0, other arithmetic: 28.9 us -> none  [hop(): return jnp.where(reached, new, before)]
    dot_general x2 -> x0, local copies, waits for them, and re-layouts: 18 us -> none  [one_block(): jnp.dot(query_block, symmetric, precision=lax.Precision.HIGHEST)]
    pallas_call x0 -> x2, Pallas kernels: none -> 14.4 us  [the longest x1 13.6 us: apply_carried(): pl.pallas_call(functools.partial(carried_kernel, HD, heads, width), out_s...]
  transfers between devices with their start and end apart: 4 -> 4, of which waited for: 4 -> 4; matrix products, arithmetic and copies ran while one was open for 4% -> 10% of each run, Pallas kernels for 0% -> 4%
where the time goes in v1:
time: 349 us; the launch traced here: 348 us
  waiting for transfers between devices  214 us (61%)
  local copies, waits for them, and re-layouts  49.6 us (14%)
  matrix products  37 us (11%)
  Pallas kernels  14.4 us (4%)
  between operations  13.7 us (4%)
  other arithmetic  11.7 us (3%)
  starting transfers between devices  7.7 us (2%)
    all_to_all x1, waiting for transfers between devices, body(): lax.all_to_all(produced.reshape(slot_count, devices * local_experts, mode...  93 us
    all_to_all x1, waiting for transfers between devices, body(): lax.all_to_all(outgoing, ('seq', 'head'), split_axis=1, concat_axis=1, ti...  67.2 us
    reduce_scatter x1, waiting for transfers between devices, body(): lax.psum_scatter(jnp.dot(attended, output_weight, preferred_element_type=...  33 us
    reshape x1, local copies, waits for them, and re-layouts, body(): expert_first.reshape(2, model_width, local_experts, piece_width)  27.7 us
    all_gather x1, waiting for transfers between devices, body(): lax.all_gather(jnp.concatenate([key_rows, value_rows], axis=1), 'seq')  21 us
    dot_general x1, matrix products, body(): jnp.einsum('ksed,gdef->gksef', grouped, first_local, preferred_element_ty...  19.5 us
    pallas_call x1, Pallas kernels, apply_carried(): pl.pallas_call(functools.partial(carried_kernel, HD, heads, width), out_s...  13.6 us
    dot_general x1, matrix products, body(): jnp.einsum('ksef,efd->ksed', hidden, second_local, preferred_element_type...  7.16 us
  transfers between devices with their start and end apart: 4, of which 4 were waited for; matrix products, arithmetic and copies ran while one was open for 10% of the time, Pallas kernels for 4%

profile of v1, /device:TPU:0, one launch (start us, length us, event | category | flops | bytes accessed | tf_op | source)
XLA Modules:
  0.0 348.3 jit_solution(2287754026867869828)
XLA Ops:
  6.5 2.2 multiply_reduce_fusion
  9.1 3.5 %fusion.24 = bf16[3,512,256]{1,2,0:T(8,128)(2,1)S(1)} fusion(bf16[3,2048,256]{2,1,0:T(8,128)(2,1)S(1)} %copy-done, f32[2048]{0:T(1024)} %param.11, f32[512]{0:T(512)S(1)} %add_rsqrt_fusion, bf16[512,2048]{1,0:T(8,128)(2,1)} %param.10), kind=kOutput, calls=%fused_computation.26 | convolution fusion | flops 1615200256 | bytes 6039552 | tf_op jit(solution)/shard_map/td,adc->atc/dot_general | solution.py:140
  13.6 3.4 copy-done.2
  17.0 13.6 %carried_state.1.carried_ref = f32[256,512]{1,0:T(8,128)S(1)} custom-call(f32[256,512]{1,0:T(8,128)S(1)} %get-tuple-element.9.q_ref, f32[8256,256]{1,0:T(8,128)S(1)} %copy-done.2), custom_call_target="tpu_custom_call" | custom-call | flops 8589934592 | bytes 8454144 | tf_op jit(solution)/shard_map/carried_state/pallas_call | solution.py:68
  30.6 21.0 %all-gather.3.cloned.1.call-done = bf16[2048,512]{0,1:T(8,128)(2,1)} async-done(((bf16[512,512]{0,1:T(8,128)(2,1)}), bf16[2048,512]{0,1:T(8,128)(2,1)}) %all-gather.3.cloned.1.call-update) | async-done | bytes 2097168 | tf_op jit(solution)/shard_map/all_gather | solution.py:158
  51.6 3.9 %copy.73 = bf16[2048,512]{1,0:T(8,128)(2,1)} copy(bf16[2048,512]{0,1:T(8,128)(2,1)} %all-gather.3.cloned.1.call-done) | data formatting | bytes 4194304 | tf_op jit(solution)/shard_map/all_gather | solution.py:158
  55.5 1.7 fusion.34
  58.4 2.1 convolution_convert_fusion.2
  60.8 2.5 convert_element_type.60
  65.6 33.0 %reduce-scatter.2.cloned.1.call-done = bf16[64,2048]{1,0:T(8,128)(2,1)} async-done(((bf16[512,2048]{1,0:T(8,128)(2,1)}), bf16[64,2048]{1,0:T(8,128)(2,1)}) %reduce-scatter.2.cloned.1.call-update) | async-done | bytes 262160 | tf_op jit(solution)/shard_map/reduce_scatter | solution.py:176
  98.6 1.3 multiply_reduce_fusion.1
  99.9 1.2 multiply_convert_fusion.1
  102.2 3.8 %copy.81 = bf16[12,64,2048]{2,0,1:T(8,128)(2,1)} copy(bf16[12,64,2048]{2,1,0:T(8,128)(2,1)S(1)} %bitcast.90) | data formatting | bytes 6291456 | tf_op jit(solution)/shard_map/reshape | solution.py:211
  106.0 3.7 %all-to-all-start = ((bf16[12,64,2048]{2,0,1:T(8,128)(2,1)}), bf16[12,64,2048]{2,0,1:T(8,128)(2,1)}, u32[]{:S(2)}, u32[]{:S(2)}) async-start(bf16[12,64,2048]{2,0,1:T(8,128)(2,1)} %copy.81), calls=%async_computation.1 | async-start | bytes 8388608 | tf_op jit(solution)/shard_map/all_to_all | solution.py:225
  109.7 27.7 %reshape.92 = bf16[2,2048,2,1024]{3,2,1,0:T(2,128)(2,1)} reshape(bf16[2,2048,2048]{2,1,0:T(8,128)(2,1)} %param.18) | data formatting | bytes 33554432 | tf_op jit(solution)/shard_map/reshape | solution.py:223
  137.4 67.2 %all-to-all-done = bf16[12,64,2048]{2,0,1:T(8,128)(2,1)} async-done(((bf16[12,64,2048]{2,0,1:T(8,128)(2,1)}), bf16[12,64,2048]{2,0,1:T(8,128)(2,1)}, u32[]{:S(2)}, u32[]{:S(2)}) %all-to-all-start) | async-done | bytes 3145760 | tf_op jit(solution)/shard_map/all_to_all | solution.py:225
  204.6 19.5 %fusion.6 = f32[2,12,32,2,1024]{4,2,0,1,3:T(8,128)S(1)} fusion(bf16[2,2048,2,1024,1]{3,2,1,0,4:T(2,128)(2,1)} %bitcast.88, bf16[12,32,2,2048,1]{3,0,2,1,4:T(8,128)(2,1)} %bitcast.14), kind=kOutput, calls=%fused_computation.13 | convolution fusion | flops 6442450944 | bytes 26214400 | tf_op jit(solution)/shard_map/ksed,gdef->gksef/dot_general | solution.py:228
  224.1 7.2 %fusion.5 = bf16[12,32,2,2048]{3,1,0,2:T(8,128)(2,1)S(1)} fusion(bf16[2,1024,2048,1]{2,1,3,0:T(8,128)(2,1)} %bitcast.92, f32[2,12,32,2,1024]{4,2,0,1,3:T(8,128)S(1)} %fusion.6), kind=kOutput, calls=%fused_computation.12 | convolution fusion | flops 3227516928 | bytes 17825792 | tf_op jit(solution)/shard_map/ksef,efd->ksed/dot_general | solution.py:232
  231.3 3.8 %copy.99 = bf16[12,32,2,2048]{3,0,2,1:T(8,128)(2,1)} copy(bf16[12,32,2,2048]{3,1,0,2:T(8,128)(2,1)S(1)} %fusion.5) | data formatting | bytes 6291456 | tf_op jit(solution)/shard_map/reshape | solution.py:236
  235.0 3.9 %all-to-all-start.1 = ((bf16[12,64,2048]{2,0,1:T(8,128)(2,1)}), bf16[12,64,2048]{2,0,1:T(8,128)(2,1)}, u32[]{:S(2)}, u32[]{:S(2)}) async-start(bf16[12,64,2048]{2,0,1:T(8,128)(2,1)} %bitcast.87), calls=%async_computation.2 | async-start | bytes 8388608 | tf_op jit(solution)/shard_map/all_to_all | solution.py:235
  239.6 1.2 select_reduce_fusion
  240.8 93.0 %all-to-all-done.1 = bf16[12,64,2048]{2,0,1:T(8,128)(2,1)} async-done(((bf16[12,64,2048]{2,0,1:T(8,128)(2,1)}), bf16[12,64,2048]{2,0,1:T(8,128)(2,1)}, u32[]{:S(2)}, u32[]{:S(2)}) %all-to-all-start.1) | async-done | bytes 3145760 | tf_op jit(solution)/shard_map/all_to_all | solution.py:235
  333.8 4.1 %copy.88 = bf16[12,64,2048]{2,1,0:T(8,128)(2,1)S(1)} copy(bf16[12,64,2048]{2,0,1:T(8,128)(2,1)} %all-to-all-done.1) | data formatting | bytes 6291456 | tf_op jit(solution)/shard_map/all_to_all | solution.py:235
  337.9 3.5 %fusion.11 = bf16[64,2048]{1,0:T(8,128)(2,1)} fusion(f32[64,768]{1,0:T(8,128)S(1)} %copy-done.6, bf16[768,2048]{1,0:T(8,128)(2,1)S(1)} %bitcast.89, bf16[64,2048]{1,0:T(8,128)(2,1)S(1)} %copy-done.4, f32[512,2048]{1,0:T(8,128)} %convert_element_type.60, s32[]{:T(128)S(6)} %select_n.11), kind=kOutput, calls=%fused_computation.15 | convolution fusion | flops 1208483840 | bytes 4390916 | tf_op jit(solution)/shard_map/dot_general | solution.py:245
  (54 shorter events, 6.6 us)
Async XLA Ops:
  6.5 2.5 copy-start
  6.5 45.0 %all-gather.3.cloned.1.call-start = ((), (), s32[]{:S(2)}) async-start(), calls=%async_computation.4 | async-start | bytes 2621440 | tf_op jit(solution)/shard_map/all_gather | solution.py:158
  13.5 85.1 %reduce-scatter.2.cloned.1.call-start = ((), (), s32[]{:S(2)}) async-start(), calls=%async_computation.3 | async-start | bytes 2359296 | tf_op jit(solution)/shard_map/reduce_scatter | solution.py:176
  13.6 3.4 copy-start.2
  57.2 1.2 copy-start.5
  58.4 2.1 copy-start.11
  58.4 2.4 copy-start.3
  60.8 39.1 %copy-start.10 = (f32[2048]{0:T(1024)S(1)}, f32[2048]{0:T(1024)}, u32[]{:S(2)}) copy-start(f32[2048]{0:T(1024)} %param.15) | copy-start | bytes 24580
  65.0 34.9 %copy-start.7 = (s32[64,8]{1,0:T(8,128)}, s32[64,8]{1,0:T(8,128)S(1)}, u32[]{:S(2)}) copy-start(s32[64,8]{1,0:T(8,128)S(1)} %add.65) | copy-start | bytes 6148
  106.0 98.6 %all-to-all-start = ((bf16[12,64,2048]{2,0,1:T(8,128)(2,1)}), bf16[12,64,2048]{2,0,1:T(8,128)(2,1)}, u32[]{:S(2)}, u32[]{:S(2)}) async-start(bf16[12,64,2048]{2,0,1:T(8,128)(2,1)} %copy.81), calls=%async_computation.1 | async-start | bytes 8388608 | tf_op jit(solution)/shard_map/all_to_all | solution.py:225
  235.0 3.9 %copy-start.9 = (bf16[2048,64]{0,1:T(8,128)(2,1)S(1)}, bf16[2048,64]{0,1:T(8,128)(2,1)}, u32[]{:S(2)}) copy-start(bf16[2048,64]{0,1:T(8,128)(2,1)} %param.16) | copy-start | bytes 786436
  235.0 4.6 %copy-start.8 = (s32[64,8]{1,0:T(8,128)S(1)}, s32[64,8]{1,0:T(8,128)}, u32[]{:S(2)}) copy-start(s32[64,8]{1,0:T(8,128)} %copy-done.7) | copy-start | bytes 6148
  235.0 98.8 %all-to-all-start.1 = ((bf16[12,64,2048]{2,0,1:T(8,128)(2,1)}), bf16[12,64,2048]{2,0,1:T(8,128)(2,1)}, u32[]{:S(2)}, u32[]{:S(2)}) async-start(bf16[12,64,2048]{2,0,1:T(8,128)(2,1)} %bitcast.87), calls=%async_computation.2 | async-start | bytes 8388608 | tf_op jit(solution)/shard_map/all_to_all | solution.py:235
  240.8 97.1 %copy-start.4 = (bf16[64,2048]{1,0:T(8,128)(2,1)S(1)}, bf16[64,2048]{1,0:T(8,128)(2,1)}, u32[]{:S(2)}) copy-start(bf16[64,2048]{1,0:T(8,128)(2,1)} %reduce-scatter.2.cloned.1.call-done) | copy-start | bytes 786436
  333.8 4.1 %copy-start.6 = (f32[64,768]{1,0:T(8,128)S(1)}, f32[64,768]{1,0:T(8,128)}, u32[]{:S(2)}) copy-start(f32[64,768]{1,0:T(8,128)} %select_reduce_fusion) | copy-start | bytes 589828
  333.8 7.6 %copy-start.1 = (bf16[3,2048,256]{2,1,0:T(8,128)(2,1)S(1)}, bf16[3,2048,256]{2,1,0:T(8,128)(2,1)}, u32[]{:S(2)}) copy-start(bf16[3,2048,256]{2,1,0:T(8,128)(2,1)} %param.12) | copy-start | bytes 9437188
Sparse Core Ops, SparseCore 0:
  13.7 37.8 all-gather.2
  60.7 37.9 reduce-scatter.1

commit v2 on v1

--- a/solution.py
+++ b/solution.py
@@ -119,6 +119,310 @@
         compiler_params=pltpu.CompilerParams(vmem_limit_bytes=40 * 2**20),
         name="causal_scores",
     )(lax.axis_index("seq").astype(jnp.int32).reshape(1), q_t, keys, values, carried)
+
+
+MESH = pl.DeviceIdType.MESH
+
+
+def flipped(index, mask):
+    bit = 1
+    while bit <= mask:
+        if mask & bit:
+            index = index + bit - 2 * bit * ((index // bit) % 2)
+        bit *= 2
+    return index
+
+
+def where_am_i():
+    shard, head = lax.axis_index("seq"), lax.axis_index("head")
+    return shard, head // 2, head % 2
+
+
+def greet(devices):
+    barrier = pltpu.get_barrier_semaphore()
+    for device in devices:
+        pl.semaphore_signal(barrier, inc=1, device_id=device, device_id_type=MESH)
+    pl.semaphore_wait(barrier, len(devices))
+
+
+def partners(shard, level, core, levels):
+    sibling = (shard, level * 2 + 1 - core)
+    across = [(flipped(shard, d), level * 2 + core) for d in (1, 2)]
+    along = [(shard, flipped(level, k) * 2 + core) for k in range(1, levels)]
+    return sibling, across, along
+
+
+def spread_kernel(levels, own_ref, all_ref, own_sem, z_send, xy_send, diag_send, twin_send, recv):
+    shard, level, core = where_am_i()
+    sibling, across, along = partners(shard, level, core, levels)
+    greet([sibling] + across + along)
+
+    def place(d, k, other):
+        mine = 1 - core if other else core
+        return flipped(shard, d) * (2 * levels) + flipped(level, k) * 2 + mine
+
+    keep = pltpu.make_async_copy(own_ref, all_ref.at[place(0, 0, 0)], own_sem)
+    keep.start()
+    started = []
+
+    def push(d, k, send_sem, recv_sem, device):
+        source = own_ref if d == 0 and k == 0 else all_ref.at[place(d, k, 0)]
+        copy = pltpu.make_async_remote_copy(
+            src_ref=source,
+            dst_ref=all_ref.at[place(d, k, 0)],
+            send_sem=send_sem,
+            recv_sem=recv_sem,
+            device_id=device,
+            device_id_type=MESH,
+        )
+        copy.start()
+        started.append(copy)
+
+    def arrive(d, k, other):
+        pltpu.make_async_remote_copy(
+            src_ref=own_ref,
+            dst_ref=all_ref.at[place(d, k, other)],
+            send_sem=z_send.at[0],
+            recv_sem=recv.at[d, k, other],
+            device_id=sibling,
+            device_id_type=MESH,
+        ).wait_recv()
+
+    for k in range(levels):
+        if k > 0:
+            arrive(0, k, 0)
+        push(0, k, xy_send.at[0, k], recv.at[1, k, 0], across[0])
+        push(0, k, xy_send.at[1, k], recv.at[2, k, 0], across[1])
+        if k == 0:
+            for far in range(1, levels):
+                push(0, 0, z_send.at[far], recv.at[0, far, 0], along[far - 1])
+        push(0, k, twin_send.at[0, k], recv.at[0, k, 1], sibling)
+    for k in range(levels):
+        for d in (1, 2):
+            arrive(d, k, 0)
+            if (k < levels // 2) == (d == 1):
+                push(d, k, diag_send.at[k], recv.at[3, k, 0], across[2 - d])
+            push(d, k, twin_send.at[d, k], recv.at[d, k, 1], sibling)
+    for k in range(levels):
+        arrive(3, k, 0)
+        push(3, k, twin_send.at[3, k], recv.at[3, k, 1], sibling)
+    for d in range(4):
+        for k in range(levels):
+            arrive(d, k, 1)
+    for copy in started:
+        copy.wait_send()
+    keep.wait()
+
+
+def spread(slab):
+    levels = lax.axis_size("head") // 2
+    dma = pltpu.SemaphoreType.DMA
+    return pl.pallas_call(
+        functools.partial(spread_kernel, levels),
+        out_shape=jax.ShapeDtypeStruct((8 * levels,) + slab.shape, slab.dtype),
+        in_specs=[pl.BlockSpec(memory_space=pl.ANY)],
+        out_specs=pl.BlockSpec(memory_space=pl.ANY),
+        scratch_shapes=[
+            dma,
+            dma((levels,)),
+            dma((2, levels)),
+            dma((levels,)),
+            dma((4, levels)),
+            dma((4, levels, 2)),
+        ],
+        compiler_params=pltpu.CompilerParams(collective_id=1, has_side_effects=True),
+        name="spread_tokens",
+    )(slab)
+
+
+def collect_kernel(
+    levels, part_ref, sum_ref, twin, diag, cross, line,
+    twin_send, diag_send, cross_send, line_send, twin_recv, diag_recv, cross_recv, line_recv,
+):
+    shard, level, core = where_am_i()
+    sibling, across, along = partners(shard, level, core, levels)
+    greet([sibling] + across + along)
+    started = []
+
+    def place(d, k, other):
+        mine = 1 - core if other else core
+        return flipped(shard, d) * (2 * levels) + flipped(level, k) * 2 + mine
+
+    def copy_of(source, target, send_sem, recv_sem, device):
+        return pltpu.make_async_remote_copy(
+            src_ref=source,
+            dst_ref=target,
+            send_sem=send_sem,
+            recv_sem=recv_sem,
+            device_id=device,
+            device_id_type=MESH,
+        )
+
+    def push(*args):
+        copy = copy_of(*args)
+        copy.start()
+        started.append(copy)
+
+    def arrive(target, recv_sem):
+        copy_of(target, target, twin_send.at[0, 0], recv_sem, sibling).wait_recv()
+
+    def paired(d, k):
+        arrive(twin.at[d, k], twin_recv.at[d, k])
+        return part_ref[place(d, k, 0)].astype(jnp.float32) + twin[d, k].astype(jnp.float32)
+
+    for d in (3, 1, 2, 0):
+        for k in reversed(range(levels)):
+            push(
+                part_ref.at[place(d, k, 1)], twin.at[d, k],
+                twin_send.at[d, k], twin_recv.at[d, k], sibling,
+            )
+    for k in reversed(range(levels)):
+        twin[3, k] = paired(3, k).astype(twin.dtype)
+        push(
+            twin.at[3, k], diag.at[k], diag_send.at[k], diag_recv.at[k],
+            across[0 if k < levels // 2 else 1],
+        )
+    for relayed in (False, True):
+        for k in reversed(range(levels)):
+            for d in (1, 2):
+                if ((k < levels // 2) == (d == 2)) != relayed:
+                    continue
+                value = paired(d, k)
+                if relayed:
+                    arrive(diag.at[k], diag_recv.at[k])
+                    value = value + diag[k].astype(jnp.float32)
+                twin[d, k] = value.astype(twin.dtype)
+                push(
+                    twin.at[d, k], cross.at[d - 1, k],
+                    cross_send.at[d - 1, k], cross_recv.at[d - 1, k], across[d - 1],
+                )
+    for k in reversed(range(levels)):
+        value = paired(0, k)
+        for side in (0, 1):
+            arrive(cross.at[side, k], cross_recv.at[side, k])
+            value = value + cross[side, k].astype(jnp.float32)
+        if k > 0:
+            twin[0, k] = value.astype(twin.dtype)
+            push(twin.at[0, k], line.at[k], line_send.at[k], line_recv.at[k], along[k - 1])
+        else:
+            sum_ref[...] = value
+    for k in range(1, levels):
+        arrive(line.at[k], line_recv.at[k])
+        sum_ref[...] += line[k].astype(jnp.float32)
+    for copy in started:
+        copy.wait_send()
+
+
+def collect(parts):
+    levels = lax.axis_size("head") // 2
+    dma = pltpu.SemaphoreType.DMA
+    slab = parts.shape[1:]
+    counts = [(4, levels), (levels,), (2, levels), (levels,)]
+    return pl.pallas_call(
+        functools.partial(collect_kernel, levels),
+        out_shape=jax.ShapeDtypeStruct(slab, jnp.float32),
+        in_specs=[pl.BlockSpec(memory_space=pltpu.VMEM)],
+        out_specs=pl.BlockSpec(memory_space=pltpu.VMEM),
+        scratch_shapes=[pltpu.VMEM(count + slab, parts.dtype) for count in counts]
+        + [dma(count) for count in counts] * 2,
+        compiler_params=pltpu.CompilerParams(
+            collective_id=2, has_side_effects=True, vmem_limit_bytes=40 * 2**20
+        ),
+        name="collect_sums",
+    )(parts)
+
+
+def expert_kernel(
+    groups, rows, span, code_rows_ref, code_ref, high_ref, low_ref, tokens_ref,
+    first_ref, second_ref, out_ref, chosen, total,
+):
+    expert, step = pl.program_id(0), pl.program_id(1)
+    width = out_ref.shape[1]
+
+    @pl.when(step == 0)
+    def _():
+        slot = lax.broadcasted_iota(jnp.int32, (rows, span), 0)
+        for g in range(groups):
+            select = jnp.where(slot == code_rows_ref[0, g : g + 1, :], 1.0, 0.0).astype(jnp.bfloat16)
+            chosen[g * rows : (g + 1) * rows, :] = jnp.dot(
+                select,
+                tokens_ref[g * span : (g + 1) * span, :width],
+                preferred_element_type=jnp.float32,
+            ).astype(jnp.bfloat16)
+        total[...] = jnp.zeros_like(total)
+
+    inputs = chosen[...]
+    gate_part = jnp.dot(inputs, first_ref[0], preferred_element_type=jnp.float32)
+    up_part = jnp.dot(inputs, first_ref[1], preferred_element_type=jnp.float32)
+    hidden = (gate_part / (1.0 + jnp.exp(-gate_part)) * up_part).astype(jnp.bfloat16)
+    total[...] += jnp.dot(hidden, second_ref[...], preferred_element_type=jnp.float32)
+
+    @pl.when(step == pl.num_programs(1) - 1)
+    def _():
+        slot = lax.broadcasted_iota(jnp.int32, (span, rows), 1)
+        for g in range(groups):
+            tokens = slice(g * span, (g + 1) * span)
+            produced = total[g * rows : (g + 1) * rows, :].astype(jnp.bfloat16)
+            hit = slot == code_ref[0, tokens, :]
+            mixed = jnp.dot(
+                jnp.where(hit, high_ref[0, tokens, :], 0.0).astype(jnp.bfloat16),
+                produced,
+                preferred_element_type=jnp.float32,
+            ) + jnp.dot(
+                jnp.where(hit, low_ref[0, tokens, :], 0.0).astype(jnp.bfloat16),
+                produced,
+                preferred_element_type=jnp.float32,
+            )
+
+            @pl.when(expert == 0)
+            def _():
+                out_ref[tokens, :] = mixed.astype(out_ref.dtype)
+
+            @pl.when(expert > 0)
+            def _():
+                out_ref[tokens, :] = (out_ref[tokens, :].astype(jnp.float32) + mixed).astype(
+                    out_ref.dtype
+                )
+
+
+def run_experts(code, high, low, rows, span, tokens, expert_first, expert_second):
+    local_experts, count = code.shape
+    width = expert_second.shape[1]
+    piece = expert_second.shape[0] // local_experts
+    chunk = min(256, piece)
+    steps = piece // chunk
+    groups = count // span
+    whole = dict(pipeline_mode=pl.Buffered(1))
+    column = pl.BlockSpec((1, count, 1), lambda e, f: (e, 0, 0), **whole)
+    return pl.pallas_call(
+        functools.partial(expert_kernel, groups, rows, span),
+        grid=(local_experts, steps),
+        out_shape=jax.ShapeDtypeStruct((count, width), jnp.bfloat16),
+        in_specs=[
+            pl.BlockSpec((1, groups, span), lambda e, f: (e, 0, 0)),
+            column,
+            column,
+            column,
+            pl.BlockSpec(tokens.shape, lambda e, f: (0, 0), **whole),
+            pl.BlockSpec((2, width, chunk), lambda e, f: (0, 0, e * steps + f)),
+            pl.BlockSpec((chunk, width), lambda e, f: (e * steps + f, 0)),
+        ],
+        out_specs=pl.BlockSpec((count, width), lambda e, f: (0, 0), **whole),
+        scratch_shapes=[
+            pltpu.VMEM((groups * rows, width), jnp.bfloat16),
+            pltpu.VMEM((groups * rows, width), jnp.float32),
+        ],
+        compiler_params=pltpu.CompilerParams(vmem_limit_bytes=52 * 2**20),
+        name="experts",
+    )(
+        code.reshape(local_experts, groups, span),
+        code[:, :, None],
+        high[:, :, None],
+        low[:, :, None],
+        tokens,
+        expert_first,
+        expert_second,
+    )
 
 
 def body(
@@ -185,66 +489,40 @@
     logits = jnp.dot(expert_input, router_weight, preferred_element_type=jnp.float32)
     matches = expert_index[:, :, None] == jnp.arange(EXPERTS, dtype=jnp.int32)
     gate_values = jax.nn.sigmoid(jnp.sum(jnp.where(matches, logits[:, None, :], 0.0), axis=2))
-    flat_matches = matches.reshape(slab_rows * TOP, EXPERTS).astype(jnp.int32)
-    earlier = jnp.cumsum(flat_matches, axis=0) - flat_matches
-    slots = jnp.sum(earlier * flat_matches, axis=1).reshape(slab_rows, TOP)
+    dense = jnp.sum(jnp.where(matches, gate_values[:, :, None], 0.0), axis=1)
+    dense_high = dense.astype(jnp.bfloat16)
+    dense_low = (dense - dense_high.astype(jnp.float32)).astype(jnp.bfloat16)
+    everyone = spread(jnp.concatenate([expert_input, dense_high, dense_low], axis=1))
     devices = lax.axis_size("seq") * lax.axis_size("head")
-    piece_count = max(1, devices // EXPERTS)
     local_experts = max(1, EXPERTS // devices)
     capacity = max(2, 3 * slab_rows * TOP // (2 * EXPERTS))
-    groups = EXPERTS * piece_count
-    targets = (slots * groups + expert_index * piece_count)[:, :, None] + jnp.arange(
-        piece_count, dtype=jnp.int32
+    slabs = max(1, 256 // slab_rows)
+    count = devices * slab_rows
+    position = lax.axis_index("seq") * lax.axis_size("head") + lax.axis_index("head")
+    mine = position * EXPERTS // devices + jnp.arange(local_experts, dtype=jnp.int32)
+    picks = (jnp.arange(EXPERTS, dtype=jnp.int32)[:, None] == mine).astype(jnp.bfloat16)
+    flat = everyone.reshape(count, -1)
+
+    def own_gates(first):
+        return lax.dot_general(
+            picks,
+            flat[:, first : first + EXPERTS],
+            (((0,), (1,)), ((), ())),
+            preferred_element_type=jnp.float32,
+        )
+
+    high, low = own_gates(model_width), own_gates(model_width + EXPERTS)
+    named = (high != 0.0).reshape(local_experts, devices, slab_rows)
+    before = jnp.tril(jnp.ones((slab_rows, slab_rows), jnp.bfloat16), -1)
+    rank = jnp.einsum(
+        "edt,ut->edu", named.astype(jnp.bfloat16), before, preferred_element_type=jnp.float32
+    ).astype(jnp.int32)
+    base = (jnp.arange(devices, dtype=jnp.int32) % slabs * capacity)[None, :, None]
+    code = jnp.where(named, base + rank, -1).reshape(local_experts, count)
+    parts = run_experts(
+        code, high, low, slabs * capacity, slabs * slab_rows, flat, expert_first, expert_second
     )
-    send_map = jnp.sum(
-        (
-            targets.reshape(slab_rows, TOP * piece_count, 1)
-            == jnp.arange(capacity * groups, dtype=jnp.int32)
-        ).astype(jnp.bfloat16),
-        axis=1,
-    )
-    outgoing = (
-        lax.dot_general(
-            send_map, expert_input, (((0,), (0,)), ((), ())), preferred_element_type=jnp.float32
-        )
-        .astype(jnp.bfloat16)
-        .reshape(capacity, groups, model_width)
-    )
-    cells = capacity * EXPERTS
-    combine_map = jnp.sum(
-        jnp.where(
-            (slots * EXPERTS + expert_index)[:, :, None] == jnp.arange(cells, dtype=jnp.int32),
-            gate_values[:, :, None],
-            0.0,
-        ),
-        axis=1,
-    )
-    piece_width = expert_first.shape[2] // local_experts
-    first_local = expert_first.reshape(2, model_width, local_experts, piece_width)
-    second_local = expert_second.reshape(local_experts, piece_width, model_width)
-    arrived = lax.all_to_all(outgoing, ("seq", "head"), split_axis=1, concat_axis=1, tiled=True)
-    slot_count = arrived.shape[0]
-    grouped = arrived.reshape(slot_count, devices, local_experts, model_width)
-    paired = jnp.einsum(
-        "ksed,gdef->gksef", grouped, first_local, preferred_element_type=jnp.float32
-    )
-    hidden = (jax.nn.silu(paired[0]) * paired[1]).astype(jnp.bfloat16)
-    produced = jnp.einsum(
-        "ksef,efd->ksed", hidden, second_local, preferred_element_type=jnp.float32
-    ).astype(jnp.bfloat16)
-    returned = lax.all_to_all(
-        produced.reshape(slot_count, devices * local_experts, model_width),
-        ("seq", "head"),
-        split_axis=1,
-        concat_axis=1,
-        tiled=True,
-    )
-    summed = jnp.sum(
-        returned.reshape(capacity, EXPERTS, piece_count, model_width).astype(jnp.float32), axis=2
-    )
-    expert_sum = jnp.dot(
-        combine_map, summed.reshape(cells, model_width), precision=lax.Precision.HIGHEST
-    )
+    expert_sum = collect(parts.reshape(devices, slab_rows, model_width))
     return (residual + expert_sum).astype(jnp.bfloat16)
 
 

time: 349 us -> 278 us (0.80)
  waiting for transfers between devices: 214 us -> 56.7 us
  Pallas kernels: 14.4 us -> 166 us
  matrix products: 37 us -> 8.77 us
  local copies, waits for them, and re-layouts: 49.6 us -> 21.7 us
  starting transfers between devices: 7.7 us -> 0.04 us
    all_to_all x2 -> x0, waiting for transfers between devices: 160 us -> none  [the longest x1 93 us: body(): lax.all_to_all(produced.reshape(slot_count, devices * local_experts, mode...]
    pallas_call x0 -> x3, Pallas kernels: none -> 151 us  [the longest x1 60.1 us: collect(): pl.pallas_call(functools.partial(collect_kernel, levels), out_shape=jax.S...]
    reshape x3 -> x1, local copies, waits for them, and re-layouts: 35.2 us -> 0.12 us  [body(): named = (high != 0.0).reshape(local_experts, devices, slab_rows)]
    dot_general x4 -> x3, matrix products: 31.2 us -> 2.94 us  [the longest x2 2.74 us: own_gates(): lax.dot_general(picks, flat[:, first:first + EXPERTS], (((0,), (1,)), (()...]
    all_to_all x2 -> x0, starting transfers between devices: 7.66 us -> none  [the longest x1 3.92 us: body(): lax.all_to_all(produced.reshape(slot_count, devices * local_experts, mode...]
    all_to_all x1 -> x0, local copies, waits for them, and re-layouts: 4.06 us -> none  [body(): lax.all_to_all(produced.reshape(slot_count, devices * local_experts, mode...]
    broadcast_in_dim x0 -> x2, local copies, waits for them, and re-layouts: none -> 4.06 us  [the longest x1 2.04 us: run_experts(): high[:, :, None]]
    another operation x1 -> x2, local copies, waits for them, and re-layouts: 0.01 us -> 3.56 us  [the longest x1 3.48 us: run_experts(): code[:, :, None]]
  transfers between devices with their start and end apart: 4 -> 2, of which waited for: 4 -> 2; matrix products, arithmetic and copies ran while one was open for 10% -> 1% of each run, Pallas kernels for 4% -> 5%
where the time goes in v2:
time: 278 us; the launch traced here: 277 us
  Pallas kernels  166 us (60%)
  waiting for transfers between devices  56.7 us (20%)
  local copies, waits for them, and re-layouts  21.7 us (8%)
  between operations  13.6 us (5%)
  other arithmetic  10.6 us (4%)
  matrix products  8.77 us (3%)
    pallas_call x1, Pallas kernels, collect(): pl.pallas_call(functools.partial(collect_kernel, levels), out_shape=jax.S...  60.1 us
    pallas_call x1, Pallas kernels, spread(): pl.pallas_call(functools.partial(spread_kernel, levels), out_shape=jax.Sh...  50.2 us
    pallas_call x1, Pallas kernels, run_experts(): pl.pallas_call(functools.partial(expert_kernel, groups, rows, span), grid...  41 us
    reduce_scatter x1, waiting for transfers between devices, body(): lax.psum_scatter(jnp.dot(attended, output_weight, preferred_element_type=...  35.6 us
    all_gather x1, waiting for transfers between devices, body(): lax.all_gather(jnp.concatenate([key_rows, value_rows], axis=1), 'seq')  21 us
    pallas_call x1, Pallas kernels, apply_carried(): pl.pallas_call(functools.partial(carried_kernel, HD, heads, width), out_s...  13.6 us
    unnamed x21, local copies, waits for them, and re-layouts  7.33 us
  transfers between devices with their start and end apart: 2, of which 2 were waited for; matrix products, arithmetic and copies ran while one was open for 1% of the time, Pallas kernels for 5%

profile of v2, /device:TPU:0, one launch (start us, length us, event | category | flops | bytes accessed | tf_op | source)
XLA Modules:
  0.0 277.2 jit_solution(9704595498423691769)
XLA Ops:
  6.5 2.2 multiply_reduce_fusion
  9.1 3.5 %fusion.9 = bf16[3,512,256]{1,2,0:T(8,128)(2,1)S(1)} fusion(bf16[3,2048,256]{2,1,0:T(8,128)(2,1)S(1)} %copy-done, f32[2048]{0:T(1024)} %param.11, f32[512]{0:T(512)S(1)} %add_rsqrt_fusion, bf16[512,2048]{1,0:T(8,128)(2,1)} %param.10), kind=kOutput, calls=%fused_computation.10 | convolution fusion | flops 1615200256 | bytes 6039552 | tf_op jit(solution)/shard_map/td,adc->atc/dot_general | solution.py:444
  12.7 0.8 pad_maximum_fusion
  13.6 3.4 %copy-done.3 = f32[8256,256]{1,0:T(8,128)S(1)} copy-done((f32[8256,256]{1,0:T(8,128)S(1)}, f32[8256,256]{1,0:T(8,128)}, u32[]{:S(2)}) %copy-start.3) | copy-done | bytes 8454168
  17.0 13.6 %carried_state.1.carried_ref = f32[256,512]{1,0:T(8,128)S(1)} custom-call(f32[256,512]{1,0:T(8,128)S(1)} %get-tuple-element.11.q_ref, f32[8256,256]{1,0:T(8,128)S(1)} %copy-done.3), custom_call_target="tpu_custom_call" | custom-call | flops 8589934592 | bytes 8454144 | tf_op jit(solution)/shard_map/carried_state/pallas_call | solution.py:68
  30.5 21.0 %all-gather.3.cloned.1.call-done = bf16[2048,512]{0,1:T(8,128)(2,1)} async-done(((bf16[512,512]{0,1:T(8,128)(2,1)}), bf16[2048,512]{0,1:T(8,128)(2,1)}) %all-gather.3.cloned.1.call-update) | async-done | bytes 2097168 | tf_op jit(solution)/shard_map/all_gather | solution.py:462
  51.5 3.9 %copy.27 = bf16[2048,512]{1,0:T(8,128)(2,1)} copy(bf16[2048,512]{0,1:T(8,128)(2,1)} %all-gather.3.cloned.1.call-done) | data formatting | bytes 4194304 | tf_op jit(solution)/shard_map/all_gather | solution.py:462
  55.5 1.8 fusion.32
  57.2 0.8 causal_scores.1
  58.2 2.1 convolution_convert_fusion
  60.4 2.5 convert_element_type.49
  63.0 35.6 %reduce-scatter.2.cloned.1.call-done = bf16[64,2048]{1,0:T(8,128)(2,1)} async-done(((bf16[512,2048]{1,0:T(8,128)(2,1)}), bf16[64,2048]{1,0:T(8,128)(2,1)}) %reduce-scatter.2.cloned.1.call-update) | async-done | bytes 262160 | tf_op jit(solution)/shard_map/reduce_scatter | solution.py:480
  98.6 1.3 multiply_reduce_fusion.1
  99.9 1.2 multiply_convert_fusion.1
  102.9 50.2 %spread_tokens.1 = bf16[32,64,2176]{2,1,0:T(8,128)(2,1)} custom-call(bf16[64,2176]{1,0:T(8,128)(2,1)} %concatenate.7.own_ref), custom_call_target="tpu_custom_call" | custom-call | tf_op jit(solution)/shard_map/spread_tokens/pallas_call | solution.py:220
  153.1 1.4 convolution_bitcast_fusion
  154.5 1.3 broadcast_compare_fusion
  156.2 3.5 %broadcast_in_dim_reshape.4.code_ref = s32[2,2048,1]{2,1,0:T(8,128)} reshape(s32[2,32,64]{2,1,0:T(8,128)S(1)} %fusion.13) | data formatting | bytes 32768 | tf_op jit(solution)/shard_map/broadcast_in_dim;reshape | solution.py:419
  159.7 2.0 copy.32.high_ref
  161.8 2.0 copy.33.low_ref
  163.8 41.0 %experts.1 = bf16[2048,2048]{1,0:T(8,128)(2,1)} custom-call(s32[2,8,256]{2,1,0:T(8,128)S(1)} %reshape_reshape.3.code_rows_ref, s32[2,2048,1]{2,1,0:T(8,128)} %broadcast_in_dim_reshape.4.code_ref, f32[2,2048,1]{2,1,0:T(8,128)} %copy.32.high_ref, f32[2,2048,1]{2,1,0:T(8,128)} %copy.33.low_ref, bf16[2048,2176]{1,0:T(8,128)(2,1)} %bitcast.45, ...), custom_call_target="tpu_custom_call" | custom-call | tf_op jit(solution)/shard_map/experts/pallas_call | solution.py:397
  204.8 3.5 %copy-done.2 = bf16[2048,2048]{1,0:T(8,128)(2,1)S(1)} copy-done((bf16[2048,2048]{1,0:T(8,128)(2,1)S(1)}, bf16[2048,2048]{1,0:T(8,128)(2,1)}, u32[]{:S(2)}) %copy-start.2) | copy-done | bytes 8388632
  208.3 60.1 %collect_sums.1 = f32[64,2048]{1,0:T(8,128)S(1)} custom-call(bf16[32,64,2048]{2,1,0:T(8,128)(2,1)S(1)} %bitcast.42), custom_call_target="tpu_custom_call" | custom-call | tf_op jit(solution)/shard_map/collect_sums/pallas_call | solution.py:321
  268.5 1.8 add_convert_fusion
  (43 shorter events, 2.8 us)
Async XLA Ops:
  6.5 2.5 copy-start
  6.5 45.0 %all-gather.3.cloned.1.call-start = ((), (), s32[]{:S(2)}) async-start(), calls=%async_computation.2 | async-start | bytes 2621440 | tf_op jit(solution)/shard_map/all_gather | solution.py:462
  13.5 85.1 %reduce-scatter.2.cloned.1.call-start = ((), (), s32[]{:S(2)}) async-start(), calls=%async_computation.1 | async-start | bytes 2359296 | tf_op jit(solution)/shard_map/reduce_scatter | solution.py:480
  13.6 3.4 %copy-start.3 = (f32[8256,256]{1,0:T(8,128)S(1)}, f32[8256,256]{1,0:T(8,128)}, u32[]{:S(2)}) copy-start(f32[8256,256]{1,0:T(8,128)} %memory_ref.1) | copy-start | bytes 25362436
  55.5 2.8 copy-start.6
  58.1 2.3 copy-start.4
  60.3 2.6 copy-start.9
  60.3 39.6 %copy-start.8 = (f32[2048]{0:T(1024)S(1)}, f32[2048]{0:T(1024)}, u32[]{:S(2)}) copy-start(f32[2048]{0:T(1024)} %param.15) | copy-start | bytes 24580
  60.4 40.8 %copy-start.7 = (bf16[2048,64]{0,1:T(8,128)(2,1)S(1)}, bf16[2048,64]{0,1:T(8,128)(2,1)}, u32[]{:S(2)}) copy-start(bf16[2048,64]{0,1:T(8,128)(2,1)} %param.16) | copy-start | bytes 786436
  204.8 65.5 %copy-start.1 = (bf16[3,2048,256]{2,1,0:T(8,128)(2,1)S(1)}, bf16[3,2048,256]{2,1,0:T(8,128)(2,1)}, u32[]{:S(2)}) copy-start(bf16[3,2048,256]{2,1,0:T(8,128)(2,1)} %param.12) | copy-start | bytes 9437188
  204.8 3.5 %copy-start.2 = (bf16[2048,2048]{1,0:T(8,128)(2,1)S(1)}, bf16[2048,2048]{1,0:T(8,128)(2,1)}, u32[]{:S(2)}) copy-start(bf16[2048,2048]{1,0:T(8,128)(2,1)} %experts.1) | copy-start | bytes 25165828
  208.3 60.2 %copy-start.5 = (bf16[64,2048]{1,0:T(8,128)(2,1)S(1)}, bf16[64,2048]{1,0:T(8,128)(2,1)}, u32[]{:S(2)}) copy-start(bf16[64,2048]{1,0:T(8,128)(2,1)} %reduce-scatter.2.cloned.1.call-done) | copy-start | bytes 786436
Sparse Core Ops, SparseCore 0:
  13.6 37.8 all-gather.2
  60.5 38.0 reduce-scatter.1
